TPU v7x, 256 devices: a whole 4x4x8 slice. The times are simulated.
256 devices in a mesh: aux: 4 (over x), blk: 32 (over z, y), occ: 2 (over core).
Axes of the slice: x: 4, y: 4, z: 8, core: 2. Of those that a mesh axis runs over, the one named last changes fastest.
Arguments:
- integrals: bfloat16 [16, 32, 11, 512, 512], P('aux', 'blk'), may hold values from -0.078125 to 0.078125
- orbitals: bfloat16 [16384, 512], P('blk', 'occ'), may hold values from -6 to 6
- pair_lists: int32 [32, 11], P('blk'), may hold values from 0 to 31, as said below
- pair_counts: int32 [32], P('blk'), may hold values from 1 to 11, as said below
Outputs:
- exchange: float32 [32, 512, 512], P('blk', 'aux')
Inputs may be any that keep to these rules, and one draw needn't show every extreme that they name: `pair_lists`: entry 0 of row m is m itself; entries past pair_counts[m] are never read. `pair_counts`: some block has all 11 slots live.
All inputs are finite; a program needn't handle non-finite values.
Results may differ from a plain program's by a relative error of at most 0.00099.
Values may be sent and summed in bfloat16 or wider, within the bound.
A program may use at most 192 MiB of HBM per device.

v0:
```python
import jax
import jax.numpy as jnp
from jax import lax
from jax.sharding import PartitionSpec as P


def slot_term(integral_block, picked):
    return jnp.einsum("pab,bi->pai", integral_block, picked, preferred_element_type=jnp.float32)


def zero_term(integral_block, picked):
    return jnp.zeros(
        (integral_block.shape[0], integral_block.shape[1], picked.shape[1]), jnp.float32
    )


def per_device(integrals, orbitals, pair_lists, pair_counts):
    local_ints = integrals[:, 0]
    width = orbitals.shape[0]
    columns = orbitals.shape[1]
    slot_total = pair_lists.shape[1]
    live = pair_counts[0]
    start_sum = jnp.zeros((local_ints.shape[0], width, columns), jnp.float32)
    coef_table = lax.all_gather(orbitals, "blk", axis=0, tiled=True)
    running = start_sum
    for slot_index in range(slot_total):
        offset = pair_lists[0, slot_index] * width
        picked = lax.dynamic_slice_in_dim(coef_table, offset, width, 0)
        running = running + lax.cond(
            slot_index < live, slot_term, zero_term, local_ints[:, slot_index], picked
        )
    halves = running.astype(jnp.bfloat16)
    occ_total = columns * lax.axis_size("occ")
    partial_value = (
        jnp.einsum("pai,pbi->ab", halves, halves, preferred_element_type=jnp.float32) / occ_total
    )
    summed = lax.psum(partial_value, ("aux", "occ"))
    kept_rows = summed.shape[0] // lax.axis_size("aux")
    result = lax.dynamic_slice_in_dim(summed, lax.axis_index("aux") * kept_rows, kept_rows, 0)
    return result[None]


def solution(mesh):
    placed = (P("aux", "blk", None, None, None), P("blk", "occ"), P("blk", None), P("blk"))
    return jax.shard_map(
        per_device, mesh=mesh, in_specs=placed, out_specs=P("blk", "aux", None), check_vma=False
    )
```

profile of v0, /device:TPU:1, one launch (start us, length us, event | category | flops | bytes accessed | tf_op | source)
XLA Modules:
  0.0 257.6 jit_solution(4063995744080289959)
XLA Ops:
  6.5 0.0 all-gather.2.cloned.1.call-start
  6.5 1.8 copy.5
  8.3 0.0 all-gather.2.cloned.1.call-update
  8.4 0.0 all-reduce.2.cloned.1.call-start
  8.4 0.0 copy-start
  8.4 19.9 %copy.12 = bf16[4,1,11,512,512]{4,3,0,2,1:T(8,128)(2,1)} copy(bf16[4,1,11,512,512]{4,3,2,1,0:T(8,128)(2,1)} %param.26) | data formatting | bytes 46137344 | tf_op args[0]
  29.0 85.9 %all-gather.2.cloned.1.call-done = bf16[16384,256]{0,1:T(8,128)(2,1)} async-done(((bf16[512,256]{0,1:T(8,128)(2,1)}), bf16[16384,256]{0,1:T(8,128)(2,1)}) %all-gather.2.cloned.1.call-update) | async-done | bytes 8388624 | tf_op jit(solution)/shard_map/all_gather | solution.py:24
  114.9 0.0 copy-done
  114.9 2.5 conditional.11
  114.9 2.4 fusion.3
  117.4 5.0 %conditional.12 = (f32[4,512,256]{1,2,0:T(8,128)}) conditional(s32[]{:T(128)} %bitcast.46, () %tuple.128, (s32[1,11]{1,0:T(1,128)S(1)}, bf16[16384,256]{0,1:T(8,128)(2,1)}, bf16[4,11,512,512]{3,2,0,1:T(8,128)(2,1)}) %tuple.176), branch_computations={%region_2.0_spmd, %region_3.0_spmd} | conditional | flops 536870912 | bytes 4456514 | solution.py:29
  117.4 0.6 slice.101
  118.6 3.8 %fusion.12 = f32[4,512,256]{1,2,0:T(8,128)} fusion(bf16[4,11,512,512]{3,2,0,1:T(8,128)(2,1)} %get-tuple-element.571, bf16[16384,256]{0,1:T(8,128)(2,1)} %get-tuple-element.569, s32[]{:T(128)S(6)} %select_n.58), kind=kOutput, calls=%fused_computation.10 | convolution fusion | flops 536870912 | bytes 4456452 | tf_op jit(solution)/shard_map/cond/branch_1_fun/pab,bi->pai/dot_general | solution.py:8
  122.4 5.0 %conditional.13 = (f32[4,512,256]{1,2,0:T(8,128)}) conditional(s32[]{:T(128)} %bitcast.47, () %tuple.129, (s32[1,11]{1,0:T(1,128)S(1)}, bf16[16384,256]{0,1:T(8,128)(2,1)}, bf16[4,11,512,512]{3,2,0,1:T(8,128)(2,1)}) %tuple.177), branch_computations={%region_4.0_spmd, %region_5.0_spmd} | conditional | flops 536870912 | bytes 4456514 | solution.py:29
  122.4 0.6 slice.103
  123.6 3.7 %fusion.21 = f32[4,512,256]{1,2,0:T(8,128)} fusion(bf16[4,11,512,512]{3,2,0,1:T(8,128)(2,1)} %get-tuple-element.574, bf16[16384,256]{0,1:T(8,128)(2,1)} %get-tuple-element.572, s32[]{:T(128)S(6)} %select_n.59), kind=kOutput, calls=%fused_computation.17 | convolution fusion | flops 536870912 | bytes 4456452 | tf_op jit(solution)/shard_map/cond/branch_1_fun/pab,bi->pai/dot_general | solution.py:8
  127.4 5.1 %conditional.14 = (f32[4,512,256]{1,2,0:T(8,128)}) conditional(s32[]{:T(128)} %bitcast.48, () %tuple.130, (s32[1,11]{1,0:T(1,128)S(1)}, bf16[16384,256]{0,1:T(8,128)(2,1)}, bf16[4,11,512,512]{3,2,0,1:T(8,128)(2,1)}) %tuple.178), branch_computations={%region_6.0_spmd, %region_7.0_spmd} | conditional | flops 536870912 | bytes 4456514 | solution.py:29
  127.4 0.6 slice.105
  128.6 3.8 %fusion.30 = f32[4,512,256]{1,2,0:T(8,128)} fusion(bf16[4,11,512,512]{3,2,0,1:T(8,128)(2,1)} %get-tuple-element.577, bf16[16384,256]{0,1:T(8,128)(2,1)} %get-tuple-element.575, s32[]{:T(128)S(6)} %select_n.60), kind=kOutput, calls=%fused_computation.24 | convolution fusion | flops 536870912 | bytes 4456452 | tf_op jit(solution)/shard_map/cond/branch_1_fun/pab,bi->pai/dot_general | solution.py:8
  132.4 1.6 conditional.15
  132.4 1.6 broadcast.27
  134.0 1.6 conditional.16
  134.0 1.6 broadcast.28
  135.6 1.6 conditional.17
  135.6 1.6 broadcast.29
  137.3 1.6 conditional.18
  137.3 1.6 broadcast.30
  138.8 1.6 conditional.19
  138.8 1.6 broadcast.31
  140.4 1.6 conditional.20
  140.4 1.6 broadcast.32
  142.0 1.6 conditional.21
  142.0 1.6 broadcast.33
  143.6 18.1 %fusion.99 = f32[512,512]{1,0:T(8,128)} fusion(f32[4,512,256]{1,2,0:T(8,128)} %get-tuple-element.609, f32[4,512,256]{1,2,0:T(8,128)} %get-tuple-element.608, f32[4,512,256]{1,2,0:T(8,128)} %get-tuple-element.607, f32[4,512,256]{1,2,0:T(8,128)} %get-tuple-element.606, f32[4,512,256]{1,2,0:T(8,128)} %get-tuple-element.605, ...), kind=kOutput, calls=%fused_computation.80 | convolution fusion | flops 542900224 | bytes 24117248 | tf_op jit(solution)/shard_map/pai,pbi->ab/dot_general | solution.py:35
  161.7 0.0 all-reduce.2.cloned.1.call-update
  161.7 87.3 %all-reduce.2.cloned.1.call-done = f32[512,512]{1,0:T(8,128)} async-done(((f32[512,512]{1,0:T(8,128)}), f32[512,512]{1,0:T(8,128)}) %all-reduce.2.cloned.1.call-update) | async-done | bytes 1048592 | tf_op jit(solution)/shard_map/psum | solution.py:37
  249.0 1.7 dynamic-slice_bitcast_fusion
Async XLA Ops:
  6.5 108.3 %all-gather.2.cloned.1.call-start = ((), (), s32[]{:S(2)}) async-start(), calls=%async_computation | async-start | bytes 8650752 | tf_op jit(solution)/shard_map/all_gather | solution.py:24
  8.4 240.7 %all-reduce.2.cloned.1.call-start = ((), (), s32[]{:S(2)}) async-start(), calls=%async_computation.1 | async-start | bytes 2097152 | tf_op jit(solution)/shard_map/psum | solution.py:37
  8.4 106.5 %copy-start = (s32[1,11]{1,0:T(1,128)S(1)}, s32[1,11]{1,0:T(1,128)}, u32[]{:S(2)}) copy-start(s32[1,11]{1,0:T(1,128)} %param.28) | copy-start | bytes 136
Sparse Core Ops, SparseCore 0:
  9.8 105.0 all-gather.1
  161.9 87.1 all-reduce.1
where the time goes:
time: 259 us; the launch traced here: 258 us
  waiting for transfers between devices  173 us (67%)
  local copies, waits for them, and re-layouts  36.2 us (14%)
  matrix products  31.9 us (12%)
  between operations  14.1 us (5%)
    psum x1, waiting for transfers between devices, per_device(): summed = lax.psum(partial_value, ('aux', 'occ'))  87.3 us
    all_gather x1, waiting for transfers between devices, per_device(): coef_table = lax.all_gather(orbitals, 'blk', axis=0, tiled=True)  85.9 us
    unnamed x4, local copies, waits for them, and re-layouts  21.7 us
    dot_general x1, matrix products, per_device(): jnp.einsum('pai,pbi->ab', halves, halves, preferred_element_type=jnp.floa...  18.1 us
    dot_general x4, matrix products, slot_term(): jnp.einsum('pab,bi->pai', integral_block, picked, preferred_element_type=...  13.8 us
    another operation x7, local copies, waits for them, and re-layouts  11.1 us
  transfers between devices with their start and end apart: 2, of which 2 were waited for; matrix products, arithmetic and copies ran while one was open for 8% of the time, Pallas kernels for 0%

commit v1 on v0

v1 whole, which is shorter than its diff:
```python
import functools

import jax
import jax.numpy as jnp
from jax import lax
from jax.experimental import pallas as pl
from jax.experimental.pallas import tpu as pltpu
from jax.sharding import PartitionSpec as P

MESH = pl.DeviceIdType.MESH
NX, NY, NZ = 4, 4, 8
BF16, F32 = jnp.bfloat16, jnp.float32

CHUNKS = (
    (0, 128, 4, "quick"),
    (128, 128, 4, "zy"),
    (256, 128, 4, "zy"),
    (384, 128, 4, "zy"),
)


def z_tree(kind):
    if kind == "quick":
        return [(1, 0), (-1, 0), (2, 0), (-2, 0), (3, 2), (-3, -2), (4, 2)]
    return [(1, 0), (-1, 0), (2, 1), (-2, -1), (3, 2), (-3, -2), (4, 3)]


def plane_tree(kind):
    edges = []
    if kind in ("quick", "zy"):
        for node, parent in [(0, None)] + z_tree(kind):
            if parent is not None:
                edges.append(((0, node), (0, parent)))
            for dy in (1, -1, 2):
                edges.append(((dy, node), (0, node)))
    else:
        for dy in (0, 1, -1, 2):
            if dy:
                edges.append(((dy, 0), (0, 0)))
            for node, parent in z_tree("fwd"):
                edges.append(((dy, node), (dy, parent)))
    return edges


def hops(node, parent):
    dy, dz = (node[0] - parent[0]) % NY, (node[1] - parent[1]) % NZ
    return min(dy, NY - dy) + min(dz, NZ - dz)


def schedule(chunks):
    events = []
    x_free = 0.0
    for c, (row, rows, share, kind) in enumerate(chunks):
        edges = plane_tree(kind)
        start = 2.0 * c
        when = {(0, 0): start}
        kids = {}
        for node, parent in edges:
            when[node] = when[parent] + 1.6 + 0.65 * hops(node, parent)
            kids.setdefault(parent, []).append(node)
        for parent, nodes in kids.items():
            events.append((when[parent], "node", c, parent, tuple(nodes)))
        done = max(when.values()) + 1.5
        x_free = max(done, x_free)
        events.append((done, "select", c))
        unit = 15.0 * rows / 512
        if share == 4:
            events.append((x_free + 2.0 + unit / 3, "forward", c))
            x_free += unit
            ready = x_free + 4.0
        elif share == 2:
            x_free += unit / 3
            ready = x_free + 2.0
        else:
            ready = done + 0.5
        for p in range(4):
            events.append((ready + 0.2 * p, "compute", c, p))
    events.sort(key=lambda e: e[0])
    return events


def kernel(
    chunks, ints_hbm, orb_hbm, lists, counts, out_ref,
    ints, orb, acc, half, part, theirs, mine, arrived, other, *refs,
):
    count = len(chunks)
    tables, lands = refs[:count], refs[count : 2 * count]
    (
        int_sem, orb_sem, root_recv, leaf_recv, plane_send, x_recv, x_send,
        core_send, core_recv, sum_send, sum_recv, last_send, last_recv,
    ) = refs[2 * count :]
    slots = ints.shape[1]
    picks = slots - 1
    x = lax.axis_index("aux")
    plane = lax.axis_index("blk")
    core = lax.axis_index("occ")
    y, z = lax.rem(plane, NY), plane // NY

    def device(dx=0, dy=0, dz=0, dc=0):
        return (
            lax.rem(x + (dx + NX), NX),
            lax.rem(z + (dz + NZ), NZ) * NY + lax.rem(y + (dy + NY), NY),
            lax.rem(core + dc, 2),
        )

    def source(dy, dz):
        return lax.rem(z + (NZ - dz), NZ) * NY + lax.rem(y + (NY - dy), NY)

    int_copies = [
        pltpu.make_async_copy(ints_hbm.at[:, 0, s], ints.at[:, s], int_sem.at[s])
        for s in range(slots)
    ]
    orb_copy = pltpu.make_async_copy(orb_hbm, orb, orb_sem)
    orb_copy.start()
    int_copies[0].start()

    partners = {(1, 0, 0, 0), (3, 0, 0, 0), (2, 0, 0, 0), (0, 0, 0, 1)}
    for _, _, _, kind in chunks:
        for node, parent in plane_tree(kind):
            dy, dz = (node[0] - parent[0]) % NY, (node[1] - parent[1]) % NZ
            partners.add((0, dy, dz, 0))
            partners.add((0, -dy % NY, -dz % NZ, 0))
    barrier = pltpu.get_barrier_semaphore()
    for dx, dy, dz, dc in sorted(partners):
        pl.semaphore_signal(
            barrier, inc=1, device_id=device(dx, dy, dz, dc), device_id_type=MESH
        )
    orb_copy.wait()
    pl.semaphore_wait(barrier, len(partners))

    def remote(src, dst, send, recv, target):
        return pltpu.make_async_remote_copy(
            src_ref=src, dst_ref=dst, send_sem=send, recv_sem=recv,
            device_id=target, device_id_type=MESH,
        )

    inner, leaves = {}, {}
    for c, (_, _, _, kind) in enumerate(chunks):
        edges = plane_tree(kind)
        parents = {parent for _, parent in edges}
        nodes = [node for node, _ in edges if node in parents]
        inner[c] = {node: i for i, node in enumerate(nodes)}
        leaves[c] = len(edges) - len(nodes)

    def share_of(c):
        row, rows, share, _ = chunks[c]
        each = rows // share
        return row, each, (x if share == 4 else lax.rem(x, share))

    def do_node(c, node, kids):
        row, each, part_index = share_of(c)
        table = tables[c]
        block = source(*node)
        if node == (0, 0):
            first = pl.multiple_of(row + part_index * each, 16)
            src = orb.at[pl.ds(first, each)]
        else:
            src = table.at[block]
            remote(
                src, src, plane_send.at[c], root_recv.at[c, inner[c][node]], device(1)
            ).wait_recv()
        for kid in kids:
            recv = (
                root_recv.at[c, inner[c][kid]] if kid in inner[c] else leaf_recv.at[c]
            )
            remote(
                src, table.at[block], plane_send.at[c], recv,
                device(0, kid[0] - node[0], kid[1] - node[1]),
            ).start()
        if node == (0, 0):
            table[block] = orb[pl.ds(first, each)]

    def half_slots(c, part_index, which):
        return lands[c].at[pl.ds(which * (picks // 2), picks // 2), part_index]

    def x_copy(c, part_index, which, recv, dx):
        ref = half_slots(c, part_index, which)
        return remote(ref, ref, x_send.at[c], x_recv.at[c, recv], device(dx))

    def do_select(c):
        _, _, part_index = share_of(c)
        share = chunks[c][2]
        table, land = tables[c], lands[c]
        group = table.at[pl.ds(0, leaves[c])]
        remote(group, group, plane_send.at[c], leaf_recv.at[c], device(1)).wait_recv()
        live = counts[0]
        for s in range(picks):
            picked = table[lists[0, s + 1]]
            land[s, part_index] = jnp.where(s + 1 < live, picked, jnp.zeros_like(picked))
        if share == 4:
            x_copy(c, part_index, 0, 0, 1).start()
            x_copy(c, part_index, 1, 1, -1).start()
            x_copy(c, part_index, 1, 2, 1).start()
            x_copy(c, part_index, 0, 3, -1).start()
        elif share == 2:
            x_copy(c, part_index, 0, 0, 1).start()
            x_copy(c, part_index, 1, 1, -1).start()

    left, right, far = (lax.rem(x + k, NX) for k in (3, 1, 2))

    def do_forward(c):
        x_copy(c, left, 0, 0, 1).wait_recv()
        x_copy(c, left, 0, 4, 1).start()
        x_copy(c, right, 1, 1, -1).wait_recv()
        x_copy(c, right, 1, 5, -1).start()

    def do_arrive(c):
        share = chunks[c][2]
        if share == 4:
            x_copy(c, left, 1, 2, 1).wait_recv()
            x_copy(c, right, 0, 3, 1).wait_recv()
            x_copy(c, far, 0, 4, 1).wait_recv()
            x_copy(c, far, 1, 5, 1).wait_recv()
        elif share == 2:
            theirs_index = lax.rem(x + 1, 2)
            x_copy(c, theirs_index, 0, 0, 1).wait_recv()
            x_copy(c, theirs_index, 1, 1, 1).wait_recv()

    def do_compute(c, p):
        row, rows, _, _ = chunks[c]
        land = lands[c]
        lhs = jnp.concatenate(
            [ints[p, s + 1, :, row : row + rows] for s in range(picks)], axis=1
        )
        rhs = land[...].reshape(picks * rows, orb.shape[1])
        acc[p] += jnp.dot(lhs, rhs, preferred_element_type=F32)

    started = False
    waited = False
    computed = set()
    for event in schedule(chunks):
        what, c = event[1], event[2]
        if what == "node":
            do_node(c, event[3], event[4])
        elif what == "select":
            do_select(c)
        elif what == "forward":
            do_forward(c)
        else:
            if not waited:
                for copy in int_copies[1:]:
                    copy.wait()
                waited = True
            if c not in computed:
                do_arrive(c)
                computed.add(c)
            do_compute(c, event[3])
        if not started:
            started = True
            for copy in int_copies[1:]:
                copy.start()
            int_copies[0].wait()
            for p in range(4):
                acc[p] = jnp.dot(ints[p, 0], orb[...], preferred_element_type=F32)

    width = orb.shape[1]
    for p in range(4):
        half[:, p * width : (p + 1) * width] = acc[p].astype(BF16)

    basis = half.shape[0]
    kept = basis // NX
    sub = kept // 2
    scale = 1.0 / (2 * width)
    order = (2, 1, 3, 0)

    def core_copy(dx):
        return remote(
            part.at[dx, 1 - core], theirs.at[dx], core_send.at[dx], core_recv.at[dx],
            device(dc=1),
        )

    def sum_copy(dx):
        return remote(
            mine.at[dx], arrived.at[dx], sum_send.at[dx], sum_recv.at[dx], device(dx)
        )

    for dx in order:
        target = lax.rem(x + dx, NX)
        rows = half[pl.ds(pl.multiple_of(target * kept, kept), kept)]
        block = lax.dot_general(
            rows, half[...], (((1,), (1,)), ((), ())), preferred_element_type=F32
        )
        part[dx] = (block * scale).reshape(2, sub, basis)
        core_copy(dx).start()
    for dx in order:
        core_copy(dx).wait_recv()
        mine[dx] = part[dx, core] + theirs[dx]
        if dx:
            sum_copy(dx).start()
    total = mine[0]
    for dx in (1, 3, 2):
        sum_copy(dx).wait_recv()
        total = total + arrived[dx]
    mine[0] = total
    last = remote(mine.at[0], other, last_send, last_recv, device(dc=1))
    last.start()
    out_ref[pl.ds(pl.multiple_of(core * sub, sub), sub)] = total
    last.wait_recv()
    out_ref[pl.ds(pl.multiple_of((1 - core) * sub, sub), sub)] = other[...]

    last.wait_send()
    for dx in order:
        core_copy(dx).wait_send()
        if dx:
            sum_copy(dx).wait_send()
    for c, (_, _, share, kind) in enumerate(chunks):
        sent = tables[c].at[pl.ds(0, len(plane_tree(kind)))]
        remote(sent, sent, plane_send.at[c], leaf_recv.at[c], device(1)).wait_send()
        if share == 4:
            sent = lands[c].at[:, pl.ds(0, 3)]
        elif share == 2:
            sent = lands[c].at[:, 0]
        if share > 1:
            remote(sent, sent, x_send.at[c], leaf_recv.at[c], device(1)).wait_send()


def per_device(integrals, orbitals, pair_lists, pair_counts):
    aux, _, slots, basis, _ = integrals.shape
    width = orbitals.shape[1]
    picks = slots - 1
    kept = basis // NX
    count = len(CHUNKS)
    blocks = NY * NZ
    dma = pltpu.SemaphoreType.DMA
    scratch = [
        pltpu.VMEM((aux, slots, basis, basis), BF16),
        pltpu.VMEM((basis, width), BF16),
        pltpu.VMEM((aux, basis, width), F32),
        pltpu.VMEM((basis, aux * width), BF16),
        pltpu.VMEM((NX, 2, kept // 2, basis), F32),
        pltpu.VMEM((NX, kept // 2, basis), F32),
        pltpu.VMEM((NX, kept // 2, basis), F32),
        pltpu.VMEM((NX, kept // 2, basis), F32),
        pltpu.VMEM((kept // 2, basis), F32),
    ]
    scratch += [pltpu.VMEM((blocks, n // g, width), BF16) for _, n, g, _ in CHUNKS]
    scratch += [pltpu.VMEM((picks, g, n // g, width), BF16) for _, n, g, _ in CHUNKS]
    scratch += [
        dma((slots,)), dma, dma((count, 32)), dma((count,)), dma((count,)),
        dma((count, 6)), dma((count,)),
        dma((NX,)), dma((NX,)), dma((NX,)), dma((NX,)), dma, dma,
    ]
    result = pl.pallas_call(
        functools.partial(kernel, CHUNKS),
        out_shape=jax.ShapeDtypeStruct((kept, basis), F32),
        in_specs=[
            pl.BlockSpec(memory_space=pl.ANY),
            pl.BlockSpec(memory_space=pl.ANY),
            pl.BlockSpec(memory_space=pltpu.SMEM),
            pl.BlockSpec(memory_space=pltpu.SMEM),
        ],
        out_specs=pl.BlockSpec(memory_space=pltpu.VMEM),
        scratch_shapes=scratch,
        name="exchange_blocks",
        compiler_params=pltpu.CompilerParams(
            collective_id=0, has_side_effects=True, vmem_limit_bytes=58 * 2**20
        ),
    )(integrals, orbitals, pair_lists, pair_counts)
    return result[None]


def solution(mesh):
    placed = (P("aux", "blk", None, None, None), P("blk", "occ"), P("blk", None), P("blk"))
    return jax.shard_map(
        per_device, mesh=mesh, in_specs=placed, out_specs=P("blk", "aux", None), check_vma=False
    )
```

time: 259 us -> 69.8 us (0.27)
  waiting for transfers between devices: 173 us -> 0 us
  Pallas kernels: 0 us -> 67.3 us
  local copies, waits for them, and re-layouts: 36.2 us -> 1.67 us
  matrix products: 31.9 us -> 0 us
  between operations: 14.1 us -> 0.66 us
    psum x1 -> x0, waiting for transfers between devices: 87.3 us -> none  [per_device(): summed = lax.psum(partial_value, ('aux', 'occ'))]
    all_gather x1 -> x0, waiting for transfers between devices: 85.9 us -> none  [per_device(): coef_table = lax.all_gather(orbitals, 'blk', axis=0, tiled=True)]
    pallas_call x0 -> x1, Pallas kernels: none -> 67.3 us  [per_device(): pl.pallas_call(functools.partial(kernel, CHUNKS), out_shape=jax.ShapeDtyp...]
    dot_general x5 -> x0, matrix products: 31.9 us -> none  [the longest x1 18.1 us: per_device(): jnp.einsum('pai,pbi->ab', halves, halves, preferred_element_type=jnp.floa...]
    unnamed x4 -> x1, local copies, waits for them, and re-layouts: 21.7 us -> 1.67 us
    another operation x7 -> x0, local copies, waits for them, and re-layouts: 11.1 us -> none
  transfers between devices with their start and end apart: 2 -> 0, of which waited for: 2 -> 0; matrix products, arithmetic and copies ran while one was open for 8% -> 0% of each run, Pallas kernels for 0% -> 0%
where the time goes in v1:
time: 69.8 us; the launch traced here: 69.6 us
  Pallas kernels  67.3 us (96%)
  local copies, waits for them, and re-layouts  1.67 us (2%)
    pallas_call x1, Pallas kernels, per_device(): pl.pallas_call(functools.partial(kernel, CHUNKS), out_shape=jax.ShapeDtyp...  67.3 us
    unnamed x1, local copies, waits for them, and re-layouts  1.67 us

profile of v1, /device:TPU:1, one launch (start us, length us, event | category | flops | bytes accessed | tf_op | source)
XLA Modules:
  0.0 69.6 jit_solution(12350272885217593121)
XLA Ops:
  0.7 67.3 %exchange_blocks.1 = f32[128,512]{1,0:T(8,128)} custom-call(bf16[4,1,11,512,512]{4,3,2,1,0:T(8,128)(2,1)} %ints_hbm.1, bf16[512,256]{1,0:T(8,128)(2,1)} %orb_hbm.1, s32[1,11]{1,0:T(1,128)} %lists.1, s32[1]{0:T(128)S(6)} %copy.6.counts), custom_call_target="tpu_custom_call" | custom-call | tf_op jit(solution)/shard_map/exchange_blocks/pallas_call | solution.py:343
  68.0 1.7 %copy.7 = f32[1,128,512]{2,1,0:T(8,128)} copy(f32[1,128,512]{2,1,0:T(8,128)} %bitcast.1) | data formatting | bytes 524288

commit v2 on v1

v2 whole, which is shorter than its diff:
```python
import functools

import jax
import jax.numpy as jnp
from jax import lax
from jax.experimental import pallas as pl
from jax.experimental.pallas import tpu as pltpu
from jax.sharding import PartitionSpec as P

MESH = pl.DeviceIdType.MESH
NX, NY, NZ = 4, 4, 8
BF16, F32 = jnp.bfloat16, jnp.float32

CHUNKS = (
    (0, 128, 4, "zy quick direct"),
    (128, 64, 4, "yz fwd fwd"),
    (192, 64, 4, "yz fwd fwd"),
    (256, 64, 4, "yz fwd direct"),
    (320, 64, 4, "yz fwd direct"),
    (384, 128, 1, "zy fwd fwd"),
)
GROUPS = ((0, 128), (128, 128), (256, 128), (384, 128))


def z_tree(kind, flip):
    if kind == "direct":
        return [(k, 0) for k in (1, -1, 2, -2, 3, -3, 4)]
    if kind == "quick":
        edges = [(1, 0), (-1, 0), (2, 0), (-2, 0), (3, 2), (-3, -2), (4, 2)]
    else:
        edges = [(1, 0), (-1, 0), (2, 1), (-2, -1), (3, 2), (-3, -2), (4, 3)]
    if flip:
        edges[-1] = (-4, -edges[-1][1])
    return edges


def y_tree(kind, flip):
    if kind == "direct":
        return [(1, 0), (-1, 0), (2, 0)]
    return [(1, 0), (-1, 0), (-2, -1) if flip else (2, 1)]


def plane_tree(kind, flip):
    first, z_kind, y_kind = kind.split()
    edges = []
    if first == "zy":
        for dz, parent in [(0, None)] + z_tree(z_kind, flip):
            if parent is not None:
                edges.append(((0, dz), (0, parent)))
        for dz, _ in [(0, None)] + z_tree(z_kind, flip):
            for dy, parent in y_tree(y_kind, flip ^ (dz & 1)):
                edges.append(((dy, dz), (parent, dz)))
    else:
        for dy, parent in y_tree(y_kind, flip):
            edges.append(((dy, 0), (parent, 0)))
        for dy, _ in [(0, None)] + y_tree(y_kind, flip):
            for dz, parent in z_tree(z_kind, flip ^ (dy & 1)):
                edges.append(((dy, dz), (dy, parent)))
    return edges


def hop_counts(node, parent):
    return node[0] - parent[0], node[1] - parent[1]


LINK = 0.011
ISSUE, FIXED, HOP = 0.05, 1.4, 0.65
PRODUCT = 1.2


def schedule(chunks):
    free = {}
    clock = 0.0
    pending = []
    arrived = {}
    waiting = [depth for _, depth in GROUPS]

    def send(way, hops, kib):
        nonlocal clock
        clock += ISSUE
        if abs(hops) == 2 and way == "y":
            ways, load = (("y", 1), ("y", -1)), 1.0
        else:
            ways, load = ((way, 1 if hops > 0 else -1),), abs(hops)
        begin = max([clock] + [free.get(w, 0.0) for w in ways])
        end = begin + load * 2 * kib * LINK
        for w in ways:
            free[w] = end
        return end + FIXED + HOP * abs(hops)

    trees = []
    for c, (row, rows, share, kind) in enumerate(chunks):
        edges = plane_tree(kind, c & 1)
        kids = {}
        for node, parent in edges:
            kids.setdefault(parent, []).append(node)
        trees.append((kids, len(edges)))
        pending.append((0.25 * c, c, ("node", c, (0, 0))))
    left = [n for _, n in trees]
    latest = [0.0] * len(chunks)
    order = []
    while pending:
        early = [e for e in pending if e[0] <= clock]
        pick = (
            min(early, key=lambda e: (e[2][0] == "compute", e[1], e[0]))
            if early
            else min(pending)
        )
        pending.remove(pick)
        clock = max(clock, pick[0]) + 0.03
        event = pick[2]
        what, c = event[0], event[1]
        if what == "compute":
            order.append(event)
            clock += PRODUCT * GROUPS[c][1] / 128 + 0.4
            continue
        row, rows, share, kind = chunks[c]
        each = rows // share
        kib = each / 2
        if what == "node":
            kids, _ = trees[c]
            nodes = kids[event[2]]
            order.append(("node", c, event[2], tuple(nodes)))
            for kid in nodes:
                dy, dz = hop_counts(kid, event[2])
                t = send("y", dy, kib) if dy else send("z", dz, kib)
                latest[c] = max(latest[c], t)
                left[c] -= 1
                if kid in kids:
                    pending.append((t, c, ("node", c, kid)))
            if left[c] == 0:
                pending.append((latest[c], c, ("select", c)))
        elif what == "select":
            order.append(event)
            clock += 0.1 + 0.004 * each
            if share == 4:
                t1, t2 = send("x", 1, 5 * kib), send("x", -1, 5 * kib)
                t3, t4 = send("x", 1, 5 * kib), send("x", -1, 5 * kib)
                arrived[c] = max(t3, t4)
                pending.append((max(t1, t2), c, ("forward", c)))
            elif share == 2:
                ready = max(send("x", 1, 5 * kib), send("x", -1, 5 * kib))
                pending.append((ready, c, ("arrive", c)))
            else:
                pending.append((clock, c, ("arrive", c)))
        elif what == "forward":
            order.append(event)
            ready = max(send("x", 1, 5 * kib), send("x", -1, 5 * kib), arrived[c])
            pending.append((ready, c, ("arrive", c)))
        else:
            order.append(event)
            for g, (first, depth) in enumerate(GROUPS):
                if first <= row < first + depth:
                    waiting[g] -= rows
                    if waiting[g] == 0:
                        pending.append((clock, g, ("compute", g)))
    return order, clock


def kernel(
    chunks, ints_hbm, orb_hbm, lists_hbm, counts_hbm, out_ref,
    ints, orb, acc, half, part, theirs, mine, arrived, other, *refs,
):
    count = len(chunks)
    tables, land = refs[:count], refs[count]
    (
        lists, counts, list_sem, int_sem, orb_sem, root_recv, leaf_recv, plane_send, x_recv, x_send,
        core_send, core_recv, sum_send, sum_recv, last_send, last_recv,
    ) = refs[count + 1 :]
    slots = ints.shape[1]
    picks = slots - 1
    x = lax.axis_index("aux")
    plane = lax.axis_index("blk")
    core = lax.axis_index("occ")
    y, z = lax.rem(plane, NY), plane // NY

    def device(dx=0, dy=0, dz=0, dc=0):
        return (
            lax.rem(x + (dx + NX), NX),
            lax.rem(z + (dz + NZ), NZ) * NY + lax.rem(y + (dy + NY), NY),
            lax.rem(core + dc, 2),
        )

    def source(dy, dz):
        return lax.rem(z + (NZ - dz), NZ) * NY + lax.rem(y + (NY - dy), NY)

    int_copies = [
        pltpu.make_async_copy(ints_hbm.at[:, 0, 0], ints.at[:, 0], int_sem.at[0])
    ]
    for c, (row, rows) in enumerate(GROUPS):
        int_copies.append(
            pltpu.make_async_copy(
                ints_hbm.at[:, 0, pl.ds(1, slots - 1), :, pl.ds(row, rows)],
                ints.at[:, pl.ds(1, slots - 1), :, pl.ds(row, rows)],
                int_sem.at[c + 1],
            )
        )
    orb_copy = pltpu.make_async_copy(orb_hbm, orb, orb_sem)
    list_copies = (
        pltpu.make_async_copy(lists_hbm, lists, list_sem.at[0]),
        pltpu.make_async_copy(counts_hbm, counts, list_sem.at[1]),
    )
    orb_copy.start()
    for copy in list_copies:
        copy.start()
    int_copies[0].start()

    partners = {(1, 0, 0, 0), (3, 0, 0, 0), (2, 0, 0, 0), (0, 0, 0, 1)}
    for c, (_, _, _, kind) in enumerate(chunks):
        for node, parent in plane_tree(kind, c & 1):
            dy, dz = (node[0] - parent[0]) % NY, (node[1] - parent[1]) % NZ
            partners.add((0, dy, dz, 0))
            partners.add((0, -dy % NY, -dz % NZ, 0))
    barrier = pltpu.get_barrier_semaphore()
    for dx, dy, dz, dc in sorted(partners):
        pl.semaphore_signal(
            barrier, inc=1, device_id=device(dx, dy, dz, dc), device_id_type=MESH
        )
    orb_copy.wait()
    for copy in list_copies:
        copy.wait()
    pl.semaphore_wait(barrier, len(partners))

    def remote(src, dst, send, recv, target):
        return pltpu.make_async_remote_copy(
            src_ref=src, dst_ref=dst, send_sem=send, recv_sem=recv,
            device_id=target, device_id_type=MESH,
        )

    inner, leaves = {}, {}
    for c, (_, _, _, kind) in enumerate(chunks):
        edges = plane_tree(kind, c & 1)
        parents = {parent for _, parent in edges}
        nodes = [node for node, _ in edges if node in parents]
        inner[c] = {node: i for i, node in enumerate(nodes)}
        leaves[c] = len(edges) - len(nodes)

    def share_of(c):
        row, rows, share, _ = chunks[c]
        each = rows // share
        return row, each, (x if share == 4 else lax.rem(x, share))

    def do_node(c, node, kids):
        row, each, part_index = share_of(c)
        table = tables[c]
        block = source(*node)
        if node == (0, 0):
            first = pl.multiple_of(row + part_index * each, 16)
            src = orb.at[pl.ds(first, each)]
        else:
            src = table.at[block]
            remote(
                src, src, plane_send.at[c], root_recv.at[c, inner[c][node]], device(1)
            ).wait_recv()
        for kid in kids:
            recv = (
                root_recv.at[c, inner[c][kid]] if kid in inner[c] else leaf_recv.at[c]
            )
            remote(
                src, table.at[block], plane_send.at[c], recv,
                device(0, kid[0] - node[0], kid[1] - node[1]),
            ).start()
        if node == (0, 0):
            table[block] = orb[pl.ds(first, each)]

    def own_rows(c, part_index):
        row, each, _ = share_of(c)
        return pl.ds(pl.multiple_of(row + part_index * each, 16), each)

    def half_slots(c, part_index, which):
        return land.at[
            pl.ds(which * (picks // 2), picks // 2), own_rows(c, part_index)
        ]

    def x_copy(c, part_index, which, recv, dx):
        ref = half_slots(c, part_index, which)
        return remote(ref, ref, x_send.at[c], x_recv.at[c, recv], device(dx))

    def do_select(c):
        _, _, part_index = share_of(c)
        share = chunks[c][2]
        table, here = tables[c], own_rows(c, part_index)
        group = table.at[pl.ds(0, leaves[c])]
        remote(group, group, plane_send.at[c], leaf_recv.at[c], device(1)).wait_recv()
        live = counts[0]
        for s in range(picks):
            picked = table[lists[0, s + 1]]
            land[s, here] = jnp.where(s + 1 < live, picked, jnp.zeros_like(picked))
        if share == 4:
            x_copy(c, part_index, 0, 0, 1).start()
            x_copy(c, part_index, 1, 1, -1).start()
            x_copy(c, part_index, 1, 2, 1).start()
            x_copy(c, part_index, 0, 3, -1).start()
        elif share == 2:
            x_copy(c, part_index, 0, 0, 1).start()
            x_copy(c, part_index, 1, 1, -1).start()

    left, right, far = (lax.rem(x + k, NX) for k in (3, 1, 2))

    def do_forward(c):
        x_copy(c, left, 0, 0, 1).wait_recv()
        x_copy(c, left, 0, 4, 1).start()
        x_copy(c, right, 1, 1, -1).wait_recv()
        x_copy(c, right, 1, 5, -1).start()

    def do_arrive(c):
        share = chunks[c][2]
        if share == 4:
            x_copy(c, left, 1, 2, 1).wait_recv()
            x_copy(c, right, 0, 3, 1).wait_recv()
            x_copy(c, far, 0, 4, 1).wait_recv()
            x_copy(c, far, 1, 5, 1).wait_recv()
        elif share == 2:
            theirs_index = lax.rem(x + 1, 2)
            x_copy(c, theirs_index, 0, 0, 1).wait_recv()
            x_copy(c, theirs_index, 1, 1, 1).wait_recv()

    def product(g, p):
        row, rows = GROUPS[g]
        lhs = jnp.concatenate(
            [ints[p, s + 1, :, row : row + rows] for s in range(picks)], axis=1
        )
        rhs = land[:, row : row + rows].reshape(picks * rows, orb.shape[1])
        return acc[p] + jnp.dot(lhs, rhs, preferred_element_type=F32)

    order, _ = schedule(chunks)
    started = False
    for event in order:
        what, c = event[0], event[1]
        if what == "node":
            do_node(c, event[2], event[3])
        elif what == "select":
            do_select(c)
        elif what == "forward":
            do_forward(c)
        elif what == "arrive":
            do_arrive(c)
        else:
            int_copies[c + 1].wait()
            if event is not order[-1]:
                for p in range(4):
                    acc[p] = product(c, p)
        if not started:
            started = True
            for copy in int_copies[1:]:
                copy.start()
            int_copies[0].wait()
            for p in range(4):
                acc[p] = jnp.dot(ints[p, 0], orb[...], preferred_element_type=F32)

    width = orb.shape[1]
    final = order[-1][1]
    for p in range(4):
        half[:, p * width : (p + 1) * width] = product(final, p).astype(BF16)

    basis = half.shape[0]
    kept = basis // NX
    sub = kept // 2
    scale = 1.0 / (2 * width)
    block = lax.dot_general(
        half[...], half[...], (((1,), (1,)), ((), ())), preferred_element_type=F32
    )
    part[...] = (block * scale).reshape(NX, 2, sub, basis)
    order = (2, 1, 3, 0)
    targets = [lax.rem(x + dx, NX) for dx in range(NX)]

    def core_copy(dx):
        return remote(
            part.at[targets[dx], 1 - core], theirs.at[dx], core_send.at[dx], core_recv.at[dx],
            device(dc=1),
        )

    def sum_copy(dx):
        return remote(
            mine.at[dx], arrived.at[dx], sum_send.at[dx], sum_recv.at[dx], device(dx)
        )

    for dx in order:
        core_copy(dx).start()
    for dx in order:
        core_copy(dx).wait_recv()
        mine[dx] = part[targets[dx], core] + theirs[dx]
        if dx:
            sum_copy(dx).start()
    total = mine[0]
    for dx in (1, 3, 2):
        sum_copy(dx).wait_recv()
        total = total + arrived[dx]
    mine[0] = total
    last = remote(mine.at[0], other, last_send, last_recv, device(dc=1))
    last.start()
    out_ref[pl.ds(pl.multiple_of(core * sub, sub), sub)] = total
    last.wait_recv()
    out_ref[pl.ds(pl.multiple_of((1 - core) * sub, sub), sub)] = other[...]

    last.wait_send()
    for dx in order:
        core_copy(dx).wait_send()
        if dx:
            sum_copy(dx).wait_send()
    for c, (_, _, share, kind) in enumerate(chunks):
        sent = tables[c].at[pl.ds(0, len(plane_tree(kind, c & 1)))]
        remote(sent, sent, plane_send.at[c], leaf_recv.at[c], device(1)).wait_send()
        if share == 4:
            sent = land.at[:, pl.ds(0, 3 * share_of(c)[1])]
        elif share == 2:
            sent = land.at[:, pl.ds(0, share_of(c)[1])]
        if share > 1:
            remote(sent, sent, x_send.at[c], leaf_recv.at[c], device(1)).wait_send()


def per_device(integrals, orbitals, pair_lists, pair_counts):
    aux, _, slots, basis, _ = integrals.shape
    width = orbitals.shape[1]
    picks = slots - 1
    kept = basis // NX
    count = len(CHUNKS)
    blocks = NY * NZ
    dma = pltpu.SemaphoreType.DMA
    scratch = [
        pltpu.VMEM((aux, slots, basis, basis), BF16),
        pltpu.VMEM((basis, width), BF16),
        pltpu.VMEM((aux, basis, width), F32),
        pltpu.VMEM((basis, aux * width), BF16),
        pltpu.VMEM((NX, 2, kept // 2, basis), F32),
        pltpu.VMEM((NX, kept // 2, basis), F32),
        pltpu.VMEM((NX, kept // 2, basis), F32),
        pltpu.VMEM((NX, kept // 2, basis), F32),
        pltpu.VMEM((kept // 2, basis), F32),
    ]
    scratch += [pltpu.VMEM((blocks, n // g, width), BF16) for _, n, g, _ in CHUNKS]
    scratch += [pltpu.VMEM((picks, basis, width), BF16)]
    scratch += [
        pltpu.SMEM((1, slots), jnp.int32), pltpu.SMEM((1,), jnp.int32), dma((2,)),
        dma((len(GROUPS) + 1,)), dma, dma((count, 32)), dma((count,)), dma((count,)),
        dma((count, 6)), dma((count,)),
        dma((NX,)), dma((NX,)), dma((NX,)), dma((NX,)), dma, dma,
    ]
    result = pl.pallas_call(
        functools.partial(kernel, CHUNKS),
        out_shape=jax.ShapeDtypeStruct((kept, basis), F32),
        in_specs=[
            pl.BlockSpec(memory_space=pl.ANY),
            pl.BlockSpec(memory_space=pl.ANY),
            pl.BlockSpec(memory_space=pl.ANY),
            pl.BlockSpec(memory_space=pl.ANY),
        ],
        out_specs=pl.BlockSpec(memory_space=pltpu.VMEM),
        scratch_shapes=scratch,
        name="exchange_blocks",
        compiler_params=pltpu.CompilerParams(
            collective_id=0, has_side_effects=True, vmem_limit_bytes=42 * 2**20
        ),
    )(integrals, orbitals, pair_lists, pair_counts)
    return result[None]


def solution(mesh):
    placed = (P("aux", "blk", None, None, None), P("blk", "occ"), P("blk", None), P("blk"))
    return jax.shard_map(
        per_device, mesh=mesh, in_specs=placed, out_specs=P("blk", "aux", None), check_vma=False
    )
```

time: 69.8 us -> 60.3 us (0.86)
  Pallas kernels: 67.3 us -> 57.2 us
    pallas_call x1, Pallas kernels: 67.3 us -> 57.2 us  [per_device(): pl.pallas_call(functools.partial(kernel, CHUNKS), out_shape=jax.ShapeDtyp...]
    unnamed x1 -> x5, local copies, waits for them, and re-layouts: 1.67 us -> 2.3 us
where the time goes in v2:
time: 60.3 us; the launch traced here: 60.2 us
  Pallas kernels  57.2 us (95%)
  local copies, waits for them, and re-layouts  2.3 us (4%)
  between operations  0.67 us (1%)
    pallas_call x1, Pallas kernels, per_device(): pl.pallas_call(functools.partial(kernel, CHUNKS), out_shape=jax.ShapeDtyp...  57.2 us
    unnamed x5, local copies, waits for them, and re-layouts  2.3 us

profile of v2, /device:TPU:1, one launch (start us, length us, event | category | flops | bytes accessed | tf_op | source)
XLA Modules:
  0.0 60.2 jit_solution(18161166191226424137)
XLA Ops:
  0.7 0.0 copy-start
  0.7 0.9 %copy-done = bf16[512,256]{1,0:T(8,128)(2,1)S(1)} copy-done((bf16[512,256]{1,0:T(8,128)(2,1)S(1)}, bf16[512,256]{1,0:T(8,128)(2,1)}, u32[]{:S(2)}) %copy-start) | copy-done | bytes 262168
  1.6 0.0 copy-start.1
  1.6 0.7 %copy-done.1 = s32[1,11]{1,0:T(1,128)S(1)} copy-done((s32[1,11]{1,0:T(1,128)S(1)}, s32[1,11]{1,0:T(1,128)}, u32[]{:S(2)}) %copy-start.1) | copy-done | bytes 68
  2.3 57.2 %exchange_blocks.1 = f32[128,512]{1,0:T(8,128)S(1)} custom-call(bf16[4,1,11,512,512]{4,3,2,1,0:T(8,128)(2,1)} %ints_hbm.1, bf16[512,256]{1,0:T(8,128)(2,1)S(1)} %copy-done, s32[1,11]{1,0:T(1,128)S(1)} %copy-done.1, s32[1]{0:T(128)S(6)} %copy.6.counts_hbm), custom_call_target="tpu_custom_call" | custom-call | tf_op jit(solution)/shard_map/exchange_blocks/pallas_call | solution.py:439
  59.5 0.7 %copy.7 = f32[1,128,512]{2,1,0:T(8,128)} copy(f32[1,128,512]{2,1,0:T(8,128)S(1)} %bitcast.1) | data formatting | bytes 524288
Async XLA Ops:
  0.7 1.0 %copy-start = (bf16[512,256]{1,0:T(8,128)(2,1)S(1)}, bf16[512,256]{1,0:T(8,128)(2,1)}, u32[]{:S(2)}) copy-start(bf16[512,256]{1,0:T(8,128)(2,1)} %orb_hbm.1) | copy-start | bytes 786436
  1.6 0.7 %copy-start.1 = (s32[1,11]{1,0:T(1,128)S(1)}, s32[1,11]{1,0:T(1,128)}, u32[]{:S(2)}) copy-start(s32[1,11]{1,0:T(1,128)} %lists_hbm.1) | copy-start | bytes 136

commit v3 on v2

--- a/solution.py
+++ b/solution.py
@@ -159,13 +159,13 @@
 
 def kernel(
     chunks, ints_hbm, orb_hbm, lists_hbm, counts_hbm, out_ref,
-    ints, orb, acc, half, part, theirs, mine, arrived, other, *refs,
+    ints, orb, acc, half, part, theirs, mine, coded, steps, other, *refs,
 ):
     count = len(chunks)
     tables, land = refs[:count], refs[count]
     (
         lists, counts, list_sem, int_sem, orb_sem, root_recv, leaf_recv, plane_send, x_recv, x_send,
-        core_send, core_recv, sum_send, sum_recv, last_send, last_recv,
+        core_send, core_recv, sum_send, sum_recv, step_send, step_recv, last_send, last_recv,
     ) = refs[count + 1 :]
     slots = ints.shape[1]
     picks = slots - 1
@@ -370,24 +370,55 @@
             device(dc=1),
         )
 
-    def sum_copy(dx):
-        return remote(
-            mine.at[dx], arrived.at[dx], sum_send.at[dx], sum_recv.at[dx], device(dx)
+    def sum_copies(dx):
+        return (
+            remote(
+                steps.at[dx, 0], steps.at[dx, 1], step_send.at[dx], step_recv.at[dx],
+                device(dx),
+            ),
+            remote(
+                coded.at[dx, 0], coded.at[dx, 1], sum_send.at[dx], sum_recv.at[dx],
+                device(dx),
+            ),
+        )
+
+    def encode(dx, value):
+        parts = []
+        for g in range(sub // 8):
+            rows = value[8 * g : 8 * g + 8]
+            top = jnp.max(jnp.abs(rows), axis=(0, 1), keepdims=True)
+            step = jnp.maximum(top, 1e-33) * (1.0 / 32000.0)
+            steps[dx, 0, g : g + 1] = jnp.broadcast_to(step, (1, 128))
+            parts.append(jnp.round(rows * (1.0 / step)).astype(jnp.int32))
+        coded[dx, 0] = jnp.concatenate(parts, axis=0).astype(jnp.int16)
+
+    def decode(dx):
+        whole = coded[dx, 1].astype(jnp.int32).astype(F32)
+        size = steps[dx, 1]
+        return jnp.concatenate(
+            [
+                whole[8 * g : 8 * g + 8] * size[g : g + 1, 0:1]
+                for g in range(sub // 8)
+            ],
+            axis=0,
         )
 
     for dx in order:
         core_copy(dx).start()
     for dx in order:
         core_copy(dx).wait_recv()
-        mine[dx] = part[targets[dx], core] + theirs[dx]
+        chip_sum = part[targets[dx], core] + theirs[dx]
         if dx:
-            sum_copy(dx).start()
-    total = mine[0]
+            encode(dx, chip_sum)
+            for copy in sum_copies(dx):
+                copy.start()
+    total = chip_sum
     for dx in (1, 3, 2):
-        sum_copy(dx).wait_recv()
-        total = total + arrived[dx]
-    mine[0] = total
-    last = remote(mine.at[0], other, last_send, last_recv, device(dc=1))
+        for copy in sum_copies(dx):
+            copy.wait_recv()
+        total = total + decode(dx)
+    mine[...] = total
+    last = remote(mine, other, last_send, last_recv, device(dc=1))
     last.start()
     out_ref[pl.ds(pl.multiple_of(core * sub, sub), sub)] = total
     last.wait_recv()
@@ -397,7 +428,8 @@
     for dx in order:
         core_copy(dx).wait_send()
         if dx:
-            sum_copy(dx).wait_send()
+            for copy in sum_copies(dx):
+                copy.wait_send()
     for c, (_, _, share, kind) in enumerate(chunks):
         sent = tables[c].at[pl.ds(0, len(plane_tree(kind, c & 1)))]
         remote(sent, sent, plane_send.at[c], leaf_recv.at[c], device(1)).wait_send()
@@ -424,8 +456,9 @@
         pltpu.VMEM((basis, aux * width), BF16),
         pltpu.VMEM((NX, 2, kept // 2, basis), F32),
         pltpu.VMEM((NX, kept // 2, basis), F32),
-        pltpu.VMEM((NX, kept // 2, basis), F32),
-        pltpu.VMEM((NX, kept // 2, basis), F32),
+        pltpu.VMEM((kept // 2, basis), F32),
+        pltpu.VMEM((NX, 2, kept // 2, basis), jnp.int16),
+        pltpu.VMEM((NX, 2, kept // 16, 128), F32),
         pltpu.VMEM((kept // 2, basis), F32),
     ]
     scratch += [pltpu.VMEM((blocks, n // g, width), BF16) for _, n, g, _ in CHUNKS]
@@ -434,7 +467,7 @@
         pltpu.SMEM((1, slots), jnp.int32), pltpu.SMEM((1,), jnp.int32), dma((2,)),
         dma((len(GROUPS) + 1,)), dma, dma((count, 32)), dma((count,)), dma((count,)),
         dma((count, 6)), dma((count,)),
-        dma((NX,)), dma((NX,)), dma((NX,)), dma((NX,)), dma, dma,
+        dma((NX,)), dma((NX,)), dma((NX,)), dma((NX,)), dma((NX,)), dma((NX,)), dma, dma,
     ]
     result = pl.pallas_call(
         functools.partial(kernel, CHUNKS),

time: 60.3 us -> 58 us (0.962)
  Pallas kernels: 57.2 us -> 54.9 us
    pallas_call x1, Pallas kernels: 57.2 us -> 54.9 us  [per_device(): pl.pallas_call(functools.partial(kernel, CHUNKS), out_shape=jax.ShapeDtyp...]
where the time goes in v3:
time: 58 us; the launch traced here: 57.8 us
  Pallas kernels  54.9 us (95%)
  local copies, waits for them, and re-layouts  2.3 us (4%)
  between operations  0.67 us (1%)
    pallas_call x1, Pallas kernels, per_device(): pl.pallas_call(functools.partial(kernel, CHUNKS), out_shape=jax.ShapeDtyp...  54.9 us
    unnamed x5, local copies, waits for them, and re-layouts  2.3 us

profile of v3, /device:TPU:1, one launch (start us, length us, event | category | flops | bytes accessed | tf_op | source)
XLA Modules:
  0.0 57.8 jit_solution(2336699790131075394)
XLA Ops:
  0.7 0.0 copy-start
  0.7 0.9 %copy-done = bf16[512,256]{1,0:T(8,128)(2,1)S(1)} copy-done((bf16[512,256]{1,0:T(8,128)(2,1)S(1)}, bf16[512,256]{1,0:T(8,128)(2,1)}, u32[]{:S(2)}) %copy-start) | copy-done | bytes 262168
  1.6 0.0 copy-start.1
  1.6 0.7 %copy-done.1 = s32[1,11]{1,0:T(1,128)S(1)} copy-done((s32[1,11]{1,0:T(1,128)S(1)}, s32[1,11]{1,0:T(1,128)}, u32[]{:S(2)}) %copy-start.1) | copy-done | bytes 68
  2.3 54.9 %exchange_blocks.1 = f32[128,512]{1,0:T(8,128)S(1)} custom-call(bf16[4,1,11,512,512]{4,3,2,1,0:T(8,128)(2,1)} %ints_hbm.1, bf16[512,256]{1,0:T(8,128)(2,1)S(1)} %copy-done, s32[1,11]{1,0:T(1,128)S(1)} %copy-done.1, s32[1]{0:T(128)S(6)} %copy.6.counts_hbm), custom_call_target="tpu_custom_call" | custom-call | tf_op jit(solution)/shard_map/exchange_blocks/pallas_call | solution.py:472
  57.1 0.7 %copy.7 = f32[1,128,512]{2,1,0:T(8,128)} copy(f32[1,128,512]{2,1,0:T(8,128)S(1)} %bitcast.1) | data formatting | bytes 524288
Async XLA Ops:
  0.7 1.0 %copy-start = (bf16[512,256]{1,0:T(8,128)(2,1)S(1)}, bf16[512,256]{1,0:T(8,128)(2,1)}, u32[]{:S(2)}) copy-start(bf16[512,256]{1,0:T(8,128)(2,1)} %orb_hbm.1) | copy-start | bytes 786436
  1.6 0.7 %copy-start.1 = (s32[1,11]{1,0:T(1,128)S(1)}, s32[1,11]{1,0:T(1,128)}, u32[]{:S(2)}) copy-start(s32[1,11]{1,0:T(1,128)} %lists_hbm.1) | copy-start | bytes 136

commit v4 on v3

--- a/solution.py
+++ b/solution.py
@@ -13,10 +13,8 @@
 
 CHUNKS = (
     (0, 128, 4, "zy quick direct"),
-    (128, 64, 4, "yz fwd fwd"),
-    (192, 64, 4, "yz fwd fwd"),
-    (256, 64, 4, "yz fwd direct"),
-    (320, 64, 4, "yz fwd direct"),
+    (128, 128, 4, "yz fwd fwd"),
+    (256, 128, 4, "yz fwd direct"),
     (384, 128, 1, "zy fwd fwd"),
 )
 GROUPS = ((0, 128), (128, 128), (256, 128), (384, 128))
@@ -63,8 +61,8 @@
     return node[0] - parent[0], node[1] - parent[1]
 
 
-LINK = 0.011
-ISSUE, FIXED, HOP = 0.05, 1.4, 0.65
+LINK = 0.01
+ISSUE, FIXED, HOP = 0.04, 1.8, 0.65
 PRODUCT = 1.2
 
 
@@ -324,7 +322,7 @@
         return acc[p] + jnp.dot(lhs, rhs, preferred_element_type=F32)
 
     order, _ = schedule(chunks)
-    started = False
+    started, roots = False, 0
     for event in order:
         what, c = event[0], event[1]
         if what == "node":
@@ -340,7 +338,8 @@
             if event is not order[-1]:
                 for p in range(4):
                     acc[p] = product(c, p)
-        if not started:
+        roots += what == "node" and event[2] == (0, 0)
+        if not started and roots == count:
             started = True
             for copy in int_copies[1:]:
                 copy.start()
@@ -482,7 +481,7 @@
         scratch_shapes=scratch,
         name="exchange_blocks",
         compiler_params=pltpu.CompilerParams(
-            collective_id=0, has_side_effects=True, vmem_limit_bytes=42 * 2**20
+            collective_id=0, has_side_effects=True, vmem_limit_bytes=214 * 2**18
         ),
     )(integrals, orbitals, pair_lists, pair_counts)
     return result[None]

time: 58 us -> 56.5 us (0.974)
  local copies, waits for them, and re-layouts: 2.3 us -> 1.35 us
    unnamed x5 -> x3, local copies, waits for them, and re-layouts: 2.3 us -> 1.35 us
where the time goes in v4:
time: 56.5 us; the launch traced here: 56.4 us
  Pallas kernels  54.4 us (96%)
  local copies, waits for them, and re-layouts  1.35 us (2%)
  between operations  0.67 us (1%)
    pallas_call x1, Pallas kernels, per_device(): pl.pallas_call(functools.partial(kernel, CHUNKS), out_shape=jax.ShapeDtyp...  54.4 us
    unnamed x3, local copies, waits for them, and re-layouts  1.35 us

profile of v4, /device:TPU:1, one launch (start us, length us, event | category | flops | bytes accessed | tf_op | source)
XLA Modules:
  0.0 56.4 jit_solution(12262716363019810171)
XLA Ops:
  0.7 0.0 copy-start
  0.7 0.6 %copy-done = s32[1,11]{1,0:T(1,128)S(1)} copy-done((s32[1,11]{1,0:T(1,128)S(1)}, s32[1,11]{1,0:T(1,128)}, u32[]{:S(2)}) %copy-start) | copy-done | bytes 68
  1.3 54.4 %exchange_blocks.1 = f32[128,512]{1,0:T(8,128)S(1)} custom-call(bf16[4,1,11,512,512]{4,3,2,1,0:T(8,128)(2,1)} %ints_hbm.1, bf16[512,256]{1,0:T(8,128)(2,1)} %orb_hbm.1, s32[1,11]{1,0:T(1,128)S(1)} %copy-done, s32[1]{0:T(128)S(6)} %copy.6.counts_hbm), custom_call_target="tpu_custom_call" | custom-call | tf_op jit(solution)/shard_map/exchange_blocks/pallas_call | solution.py:471
  55.7 0.7 %copy.7 = f32[1,128,512]{2,1,0:T(8,128)} copy(f32[1,128,512]{2,1,0:T(8,128)S(1)} %bitcast.1) | data formatting | bytes 524288
Async XLA Ops:
  0.7 0.7 %copy-start = (s32[1,11]{1,0:T(1,128)S(1)}, s32[1,11]{1,0:T(1,128)}, u32[]{:S(2)}) copy-start(s32[1,11]{1,0:T(1,128)} %lists_hbm.1) | copy-start | bytes 136

commit v5 on v4

--- a/solution.py
+++ b/solution.py
@@ -391,13 +391,13 @@
             parts.append(jnp.round(rows * (1.0 / step)).astype(jnp.int32))
         coded[dx, 0] = jnp.concatenate(parts, axis=0).astype(jnp.int16)
 
-    def decode(dx):
-        whole = coded[dx, 1].astype(jnp.int32).astype(F32)
+    def decode(dx, first, rows):
+        whole = coded[dx, 1, first : first + rows].astype(jnp.int32).astype(F32)
         size = steps[dx, 1]
         return jnp.concatenate(
             [
-                whole[8 * g : 8 * g + 8] * size[g : g + 1, 0:1]
-                for g in range(sub // 8)
+                whole[8 * g : 8 * g + 8] * size[first // 8 + g : first // 8 + g + 1, 0:1]
+                for g in range(rows // 8)
             ],
             axis=0,
         )
@@ -411,19 +411,33 @@
             encode(dx, chip_sum)
             for copy in sum_copies(dx):
                 copy.start()
-    total = chip_sum
     for dx in (1, 3, 2):
         for copy in sum_copies(dx):
             copy.wait_recv()
-        total = total + decode(dx)
-    mine[...] = total
-    last = remote(mine, other, last_send, last_recv, device(dc=1))
-    last.start()
-    out_ref[pl.ds(pl.multiple_of(core * sub, sub), sub)] = total
-    last.wait_recv()
-    out_ref[pl.ds(pl.multiple_of((1 - core) * sub, sub), sub)] = other[...]
-
-    last.wait_send()
+    parts, rows = 2, sub // 2
+    lasts = []
+    for n in range(parts):
+        first = n * rows
+        total = chip_sum[first : first + rows]
+        for dx in (1, 3, 2):
+            total = total + decode(dx, first, rows)
+        mine[first : first + rows] = total
+        last = remote(
+            mine.at[pl.ds(first, rows)], other.at[pl.ds(first, rows)],
+            last_send.at[n], last_recv.at[n], device(dc=1),
+        )
+        last.start()
+        lasts.append(last)
+        out_ref[pl.ds(pl.multiple_of(core * sub + first, 8), rows)] = total
+    for n, last in enumerate(lasts):
+        first = n * rows
+        last.wait_recv()
+        out_ref[pl.ds(pl.multiple_of((1 - core) * sub + first, 8), rows)] = other[
+            first : first + rows
+        ]
+
+    for last in lasts:
+        last.wait_send()
     for dx in order:
         core_copy(dx).wait_send()
         if dx:
@@ -466,7 +480,7 @@
         pltpu.SMEM((1, slots), jnp.int32), pltpu.SMEM((1,), jnp.int32), dma((2,)),
         dma((len(GROUPS) + 1,)), dma, dma((count, 32)), dma((count,)), dma((count,)),
         dma((count, 6)), dma((count,)),
-        dma((NX,)), dma((NX,)), dma((NX,)), dma((NX,)), dma((NX,)), dma((NX,)), dma, dma,
+        dma((NX,)), dma((NX,)), dma((NX,)), dma((NX,)), dma((NX,)), dma((NX,)), dma((2,)), dma((2,)),
     ]
     result = pl.pallas_call(
         functools.partial(kernel, CHUNKS),

time: 56.5 us -> 56.5 us (level)
  no operation moved by 1% of the time
where the time goes in v5:
time: 56.5 us; the launch traced here: 56.4 us
  Pallas kernels  54.3 us (96%)
  local copies, waits for them, and re-layouts  1.35 us (2%)
  between operations  0.67 us (1%)
    pallas_call x1, Pallas kernels, per_device(): pl.pallas_call(functools.partial(kernel, CHUNKS), out_shape=jax.ShapeDtyp...  54.3 us
    unnamed x3, local copies, waits for them, and re-layouts  1.35 us

profile of v5, /device:TPU:1, one launch (start us, length us, event | category | flops | bytes accessed | tf_op | source)
XLA Modules:
  0.0 56.4 jit_solution(4085309914899580999)
XLA Ops:
  0.7 0.0 copy-start
  0.7 0.6 %copy-done = s32[1,11]{1,0:T(1,128)S(1)} copy-done((s32[1,11]{1,0:T(1,128)S(1)}, s32[1,11]{1,0:T(1,128)}, u32[]{:S(2)}) %copy-start) | copy-done | bytes 68
  1.3 54.3 %exchange_blocks.1 = f32[128,512]{1,0:T(8,128)S(1)} custom-call(bf16[4,1,11,512,512]{4,3,2,1,0:T(8,128)(2,1)} %ints_hbm.1, bf16[512,256]{1,0:T(8,128)(2,1)} %orb_hbm.1, s32[1,11]{1,0:T(1,128)S(1)} %copy-done, s32[1]{0:T(128)S(6)} %copy.6.counts_hbm), custom_call_target="tpu_custom_call" | custom-call | tf_op jit(solution)/shard_map/exchange_blocks/pallas_call | solution.py:485
  55.7 0.7 %copy.7 = f32[1,128,512]{2,1,0:T(8,128)} copy(f32[1,128,512]{2,1,0:T(8,128)S(1)} %bitcast.1) | data formatting | bytes 524288
Async XLA Ops:
  0.7 0.7 %copy-start = (s32[1,11]{1,0:T(1,128)S(1)}, s32[1,11]{1,0:T(1,128)}, u32[]{:S(2)}) copy-start(s32[1,11]{1,0:T(1,128)} %lists_hbm.1) | copy-start | bytes 136
